TPU v7x, 256 devices: a whole 4x4x8 slice. The times are simulated.
256 devices in a mesh: batch: 32 (over x, y, core), tensor: 8 (over z).
Axes of the slice: x: 4, y: 4, z: 8, core: 2. Of those that a mesh axis runs over, the one named last changes fastest.
Arguments:
- tokens: bfloat16 [4, 128, 8192], P(None, None, 'batch'), may hold values from -96 to 96, as said below
- attn_gain: bfloat16 [8192], P('batch'), may hold values from 0.099609375 to 1.8984375
- w_query: bfloat16 [8192, 8192], P('batch', 'tensor'), may hold values from -0.0625 to 0.0625
- query_gain: bfloat16 [128], replicated, may hold values from 0.099609375 to 1.8984375
- keys: bfloat16 [32, 8, 6400, 128], P('batch', 'tensor'), may hold values from -260 to 260
- values: bfloat16 [32, 8, 6400, 128], P('batch', 'tensor'), may hold values from -18 to 18
- w_out: bfloat16 [8192, 8192], P('tensor', 'batch'), may hold values from -0.0625 to 0.0625
- ffn_gain: bfloat16 [8192], P('batch'), may hold values from 0.099609375 to 1.8984375
- w_gate: bfloat16 [8192, 28672], P('batch', 'tensor'), may hold values from -0.0625 to 0.0625
- w_up: bfloat16 [8192, 28672], P('batch', 'tensor'), may hold values from -0.0625 to 0.0625
- w_down: bfloat16 [28672, 8192], P('tensor', 'batch'), may hold values from -0.03125 to 0.03125
- citers: int32 [32, 15], P('batch'), may hold values from -1 to 127, as said below
- cite_owner: int32 [128, 2], P('batch'), may hold values from 0 to 31, as said below
- cite_slot: int32 [128, 2], P('batch'), may hold values from 0 to 14, as said below
Outputs:
- mixed: bfloat16 [4, 128, 8192], P(None, 'tensor', 'batch')
Inputs may be any that keep to these rules, and one draw needn't show every extreme that they name: `tokens`: features have scales that differ from column to column and from row to row. `citers`: row i lists in slots 0 to n - 1 the n distinct requests that cite image i, and -1 in its other slots; every image is cited by 1 to 15 requests, and some image by exactly 15. A request's 2 citations name different images; request r appears in the list of image cite_owner[r, c]. citers[cite_owner[r, c], cite_slot[r, c]] = r.
All inputs are finite; a program needn't handle non-finite values.
Results may differ from a plain program's by a relative error of at most 0.013.
Values may be sent and summed in bfloat16 or wider, within the bound.
No kernel may reach another device: no remote copies, remote signals or barrier semaphores. Data moves between devices by JAX's collectives and lax.ppermute only.
A program may use at most 128 MiB of HBM per device.

v0:
```python
import math

import jax
import jax.numpy as jnp
from jax import lax
from jax.sharding import PartitionSpec as P

EPS = 1e-05


def scale_rows(values_in, total_sq, width, gain):
    return values_in * lax.rsqrt(total_sq / width + EPS)[..., None] * gain.astype(jnp.float32)


def head_norm(query, head_dim, query_gain):
    shaped = query.reshape(query.shape[0], query.shape[1], -1, head_dim)
    power = jnp.mean(shaped * shaped, axis=-1, keepdims=True)
    return (shaped * lax.rsqrt(power + EPS) * query_gain.astype(jnp.float32)).astype(jnp.bfloat16)


def image_partials(listed, queries, image_keys, image_values):
    kv_local, head_dim = (image_keys.shape[0], image_keys.shape[2])
    slots, steps_count, heads_local = (listed.shape[0], queries.shape[1], queries.shape[2])
    group = heads_local // kv_local
    picked = queries[jnp.maximum(listed, 0)].reshape(slots, steps_count, kv_local, group, head_dim)
    scores = jnp.einsum("lsgqd,gkd->glsqk", picked, image_keys, preferred_element_type=jnp.float32)
    scores = scores * (1.0 / math.sqrt(head_dim))
    top = jnp.max(scores, axis=-1)
    weights = jnp.exp(scores - top[..., None])
    total = jnp.sum(weights, axis=-1)
    weights_low = weights.astype(jnp.bfloat16)
    numer = jnp.einsum(
        "glsqk,gkd->lsgqd", weights_low, image_values, preferred_element_type=jnp.float32
    )
    total_t = jnp.transpose(total, (1, 2, 0, 3))
    part = (
        (numer / total_t[..., None])
        .reshape(slots, steps_count, heads_local * head_dim)
        .astype(jnp.bfloat16)
    )
    lse = jnp.transpose(top, (1, 2, 0, 3)).reshape(slots, steps_count, heads_local)
    lse = lse + jnp.log(total_t.reshape(slots, steps_count, heads_local))
    lse_high = lax.optimization_barrier(lse.astype(jnp.bfloat16))
    lse_low = (lse - lse_high.astype(jnp.float32)).astype(jnp.bfloat16)
    return (part, jnp.concatenate([lse_high, lse_low], axis=-1))


def per_device(
    tokens,
    attn_gain,
    w_query,
    query_gain,
    keys,
    values,
    w_out,
    ffn_gain,
    w_gate,
    w_up,
    w_down,
    citers,
    cite_owner,
    cite_slot,
):
    n_batch = lax.axis_size("batch")
    n_tensor = lax.axis_size("tensor")
    reqs = tokens.shape[1]
    share_rows = reqs // n_batch
    full_width = tokens.shape[2] * n_batch
    head_dim = query_gain.shape[0]
    rows_x = jnp.transpose(tokens, (1, 0, 2)).astype(jnp.float32)
    normed = (rows_x * attn_gain.astype(jnp.float32)).astype(jnp.bfloat16)
    piece = normed
    own_query = lax.psum_scatter(
        jnp.einsum("rsd,dc->rsc", piece, w_query, preferred_element_type=jnp.float32),
        "batch",
        scatter_dimension=0,
        tiled=True,
    )
    queries = lax.all_gather(
        head_norm(own_query, head_dim, query_gain), "batch", axis=0, tiled=True
    )
    part, lse_both = image_partials(citers[0], queries, keys[0], values[0])
    slots = citers.shape[1]
    all_parts, all_lse = (
        lax.all_gather(part, "batch", axis=0, tiled=True),
        lax.all_gather(lse_both, "batch", axis=0, tiled=True),
    )
    flat = cite_owner * slots + cite_slot
    heads_local = all_lse.shape[-1] // 2
    chosen = all_parts[flat].astype(jnp.float32)
    picked_lse = all_lse[flat].astype(jnp.float32)
    level = picked_lse[..., :heads_local] + picked_lse[..., heads_local:]
    peak = jnp.max(level, axis=1, keepdims=True)
    share = jnp.exp(level - peak)
    share = share / jnp.sum(share, axis=1, keepdims=True)
    steps_count = chosen.shape[2]
    shaped = chosen.reshape(chosen.shape[0], chosen.shape[1], steps_count, -1, head_dim)
    attended = (
        jnp.sum(share[..., None] * shaped, axis=1)
        .reshape(share_rows, steps_count, -1)
        .astype(jnp.bfloat16)
    )
    heads_part = jnp.einsum(
        "rsc,cd->rsd",
        lax.all_gather(attended, "batch", axis=0, tiled=True),
        w_out,
        preferred_element_type=jnp.float32,
    )
    attn_out = lax.psum(heads_part, "tensor")
    resid = rows_x + attn_out
    second_sq = lax.psum(jnp.sum(resid * resid, axis=-1), "batch")
    normed_ffn = scale_rows(resid, second_sq, full_width, ffn_gain).astype(jnp.bfloat16)
    ff_local = w_gate.shape[1]
    piece = normed_ffn
    gated = jnp.einsum("rsd,df->rsf", piece, w_gate, preferred_element_type=jnp.float32)
    lifted = jnp.einsum("rsd,df->rsf", piece, w_up, preferred_element_type=jnp.float32)
    both = lax.psum_scatter(
        jnp.concatenate([gated, lifted], axis=-1).astype(jnp.bfloat16),
        "batch",
        scatter_dimension=0,
        tiled=True,
    ).astype(jnp.float32)
    hidden = (jax.nn.silu(both[..., :ff_local]) * both[..., ff_local:]).astype(jnp.bfloat16)
    down_part = jnp.einsum(
        "rsf,fd->rsd",
        lax.all_gather(hidden, "batch", axis=0, tiled=True),
        w_down,
        preferred_element_type=jnp.float32,
    )
    down_share = lax.psum_scatter(down_part, "tensor", scatter_dimension=0, tiled=True)
    out_rows = reqs // n_tensor
    base = lax.dynamic_slice_in_dim(resid, lax.axis_index("tensor") * out_rows, out_rows, 0)
    return jnp.transpose((base + down_share).astype(jnp.bfloat16), (1, 0, 2))


def solution(mesh):
    return jax.shard_map(
        per_device,
        mesh=mesh,
        in_specs=(
            P(None, None, "batch"),
            P("batch"),
            P("batch", "tensor"),
            P(),
            P("batch", "tensor", None, None),
            P("batch", "tensor", None, None),
            P("tensor", "batch"),
            P("batch"),
            P("batch", "tensor"),
            P("batch", "tensor"),
            P("tensor", "batch"),
            P("batch", None),
            P("batch", None),
            P("batch", None),
        ),
        out_specs=P(None, "tensor", "batch"),
        check_vma=False,
    )
```

profile of v0, /device:TPU:4, one launch (start us, length us, event | category | flops | bytes accessed | tf_op | source)
XLA Modules:
  0.0 671.2 jit_solution(5088814607501755807)
XLA Ops:
  7.4 2.9 fusion.35
  11.7 118.8 %all-reduce.8.cloned.1.call-done = f32[128,4,1024]{2,0,1:T(8,128)} async-done(((f32[128,4,1024]{2,0,1:T(8,128)}), f32[128,4,1024]{2,0,1:T(8,128)}) %all-reduce.8.cloned.1.call-update) | async-done | bytes 2097168
  130.5 1.5 constant_dynamic-slice_fusion
  133.8 46.9 %all-gather.5.cloned.1.call-done = bf16[128,4,8,128]{3,2,0,1:T(8,128)(2,1)} async-done(((bf16[4,4,8,128]{3,2,0,1:T(8,128)(2,1)}), bf16[128,4,8,128]{3,2,0,1:T(8,128)(2,1)}) %all-gather.5.cloned.1.call-update) | async-done | bytes 1048592 | tf_op jit(solution)/shard_map/all_gather | solution.py:79
  180.7 2.5 gather_fusion
  183.2 2.7 multiply_reduce_fusion
  185.9 2.1 fusion.1
  188.1 2.2 fusion.27
  191.4 24.2 %all_gather.16 = bf16[480,4,16]{2,1,0:T(4,128)(2,1)S(1)} all-gather(bf16[15,4,16]{2,1,0:T(4,128)(2,1)S(1)} %pad_maximum_fusion.1), channel_id=1, replica_groups=mesh['batch'=32,'tensor'=8] {'batch'}, dimensions={0}, use_global_device_ids=true | all-gather | bytes 63360 | tf_op jit(solution)/shard_map/all_gather | solution.py:86
  216.5 25.7 %all-gather.7.cloned.1.call-done = bf16[480,4,1024]{2,1,0:T(4,128)(2,1)} async-done(((bf16[15,4,1024]{2,1,0:T(4,128)(2,1)}), bf16[480,4,1024]{2,1,0:T(4,128)(2,1)}) %all-gather.7.cloned.1.call-update) | async-done | bytes 3932176 | tf_op jit(solution)/shard_map/all_gather | solution.py:85
  242.2 2.7 gather_fusion.2
  245.7 47.6 %all-gather.9.cloned.1.call-done = bf16[128,4,1024]{2,1,0:T(4,128)(2,1)} async-done(((bf16[4,4,1024]{2,1,0:T(4,128)(2,1)}), bf16[128,4,1024]{2,1,0:T(4,128)(2,1)}) %all-gather.9.cloned.1.call-update) | async-done | bytes 1048592 | tf_op jit(solution)/shard_map/all_gather | solution.py:105
  293.4 2.7 fusion.32
  296.2 73.3 %all-reduce.6.cloned.1.call-done = f32[128,4,256]{2,0,1:T(8,128)} async-done(((f32[128,4,256]{2,0,1:T(8,128)}), f32[128,4,256]{2,0,1:T(8,128)}) %all-reduce.6.cloned.1.call-update) | async-done | bytes 524304 | tf_op jit(solution)/shard_map/psum | solution.py:109
  369.5 1.2 multiply_reduce_fusion.1
  370.7 53.2 %psum.15 = f32[128,4]{0,1:T(4,128)S(1)} all-reduce(f32[128,4]{0,1:T(4,128)S(1)} %get-tuple-element.5), channel_id=1, replica_groups=mesh['batch'=32,'tensor'=8] {'batch'}, use_global_device_ids=true, to_apply=%region_9.0 | all-reduce | flops 512 | bytes 4096 | tf_op jit(solution)/shard_map/psum | solution.py:111
  423.9 3.1 convolution_convert_fusion.1
  426.9 3.1 convolution_convert_fusion
  430.0 6.9 %pad_maximum_fusion = bf16[128,4,7168]{2,0,1:T(8,128)(2,1)} fusion(bf16[128,4,3584]{2,0,1:T(8,128)(2,1)} %convolution_convert_fusion, bf16[128,4,3584]{2,0,1:T(8,128)(2,1)} %convolution_convert_fusion.1), kind=kLoop, calls=%fused_computation.7 | loop fusion | flops 14680064 | bytes 14680064 | tf_op jit(solution)/shard_map/concatenate | solution.py:118
  436.9 130.6 %all-reduce.10.cloned.1.call-done = bf16[128,4,7168]{2,0,1:T(8,128)(2,1)} async-done(((bf16[128,4,7168]{2,0,1:T(8,128)(2,1)}), bf16[128,4,7168]{2,0,1:T(8,128)(2,1)}) %all-reduce.10.cloned.1.call-update) | async-done | bytes 7340048
  569.6 51.1 %all-gather.11.cloned.1.call-done = bf16[128,4,3584]{2,1,0:T(4,128)(2,1)} async-done(((bf16[4,4,3584]{2,1,0:T(4,128)(2,1)}), bf16[128,4,3584]{2,1,0:T(4,128)(2,1)}) %all-gather.11.cloned.1.call-update) | async-done | bytes 3670032 | tf_op jit(solution)/shard_map/all_gather | solution.py:126
  620.7 4.6 fusion.4
  625.3 37.6 %reduce-scatter.4.cloned.1.call-done = f32[16,4,256]{2,0,1:T(8,128)} async-done(((f32[128,4,256]{2,0,1:T(8,128)}), f32[16,4,256]{2,0,1:T(8,128)}) %reduce-scatter.4.cloned.1.call-update) | async-done | bytes 65552 | tf_op jit(solution)/shard_map/reduce_scatter | solution.py:130
  662.9 1.5 fusion.42
  (70 shorter events, 8.2 us)
Async XLA Ops:
  6.5 417.3 %copy-start = (bf16[256,3584]{1,0:T(8,128)(2,1)S(1)}, bf16[256,3584]{1,0:T(8,128)(2,1)}, u32[]{:S(2)}) copy-start(bf16[256,3584]{1,0:T(8,128)(2,1)} %param.22) | copy-start | bytes 5505028
  6.5 3.9 copy-start.11
  6.5 3.9 copy-start.8
  6.5 127.2 %copy-start.9 = (s32[1,15]{1,0:T(1,128)S(1)}, s32[1,15]{1,0:T(1,128)}, u32[]{:S(2)}) copy-start(s32[1,15]{1,0:T(1,128)} %param.25) | copy-start | bytes 184
  6.5 176.6 %copy-start.2 = (bf16[1,1,6400,128]{3,2,1,0:T(8,128)(2,1)S(1)}, bf16[1,1,6400,128]{3,2,1,0:T(8,128)(2,1)}, u32[]{:S(2)}) copy-start(bf16[1,1,6400,128]{3,2,1,0:T(8,128)(2,1)} %param.18) | copy-start | bytes 4915204
  6.5 123.9 %all-reduce.8.cloned.1.call-start = ((), (), s32[]{:S(2)}) async-start(), calls=%async_computation.7 | async-start | bytes 4194304
  10.4 170.3 %all-gather.5.cloned.1.call-start = ((), (), s32[]{:S(2)}) async-start(), calls=%async_computation.1 | async-start | bytes 1081344 | tf_op jit(solution)/shard_map/all_gather | solution.py:79
  133.7 108.4 %all-gather.7.cloned.1.call-start = ((), (), s32[]{:S(2)}) async-start(), calls=%async_computation.2 | async-start | bytes 4055040 | tf_op jit(solution)/shard_map/all_gather | solution.py:85
  185.9 2.2 copy-start.3
  188.1 3.0 copy-start.5
  188.1 3.0 copy-start.6
  188.1 105.3 %copy-start.7 = (bf16[1024,256]{1,0:T(8,128)(2,1)S(1)}, bf16[1024,256]{1,0:T(8,128)(2,1)}, u32[]{:S(2)}) copy-start(bf16[1024,256]{1,0:T(8,128)(2,1)} %param.20) | copy-start | bytes 1572868
  190.3 105.9 %copy-start.10 = (bf16[256]{0:T(256)(128)(2,1)S(1)}, bf16[256]{0:T(256)(128)(2,1)}, u32[]{:S(2)}) copy-start(bf16[256]{0:T(256)(128)(2,1)} %param.21) | copy-start | bytes 1540
  190.3 179.2 %copy-start.4 = (bf16[4,128,256]{2,1,0:T(8,128)(2,1)S(1)}, bf16[4,128,256]{2,1,0:T(8,128)(2,1)}, u32[]{:S(2)}) copy-start(bf16[4,128,256]{2,1,0:T(8,128)(2,1)} %param.14) | copy-start | bytes 786436
  191.0 102.4 %all-gather.9.cloned.1.call-start = ((), (), s32[]{:S(2)}) async-start(), calls=%async_computation.3 | async-start | bytes 1081344 | tf_op jit(solution)/shard_map/all_gather | solution.py:105
  245.7 123.8 %all-reduce.6.cloned.1.call-start = ((), (), s32[]{:S(2)}) async-start(), calls=%async_computation.4 | async-start | bytes 1048576 | tf_op jit(solution)/shard_map/psum | solution.py:109
  296.1 271.4 %all-reduce.10.cloned.1.call-start = ((), (), s32[]{:S(2)}) async-start(), calls=%async_computation.8 | async-start | bytes 14680064
  423.9 3.1 copy-start.1
  436.9 183.8 %all-gather.11.cloned.1.call-start = ((), (), s32[]{:S(2)}) async-start(), calls=%async_computation.5 | async-start | bytes 3784704 | tf_op jit(solution)/shard_map/all_gather | solution.py:126
  569.5 93.4 %reduce-scatter.4.cloned.1.call-start = ((), (), s32[]{:S(2)}) async-start(), calls=%async_computation.6 | async-start | bytes 589824 | tf_op jit(solution)/shard_map/reduce_scatter | solution.py:130
Sparse Core Ops, SparseCore 0:
  10.7 119.7 all-reduce.7
  133.9 46.8 all-gather.4
  191.1 51.0 all-gather.6
  245.8 47.5 all-gather.8
  296.3 73.1 all-reduce.5
  437.0 130.5 all-reduce.9
  570.4 50.1 all-gather.10
  625.4 37.4 reduce-scatter.3
where the time goes:
time: 672 us; the launch traced here: 671 us
  waiting for transfers between devices  532 us (79%)
  blocking collectives  77.4 us (12%)
  matrix products  21.3 us (3%)
  other arithmetic  15.1 us (2%)
  between operations  14.4 us (2%)
  local copies, waits for them, and re-layouts  11 us (2%)
    unnamed x10, waiting for transfers between devices  250 us
    psum x1, waiting for transfers between devices, per_device(): attn_out = lax.psum(heads_part, 'tensor')  73.3 us
    psum x1, blocking collectives, per_device(): second_sq = lax.psum(jnp.sum(resid * resid, axis=-1), 'batch')  53.2 us
    all_gather x1, waiting for transfers between devices, per_device(): lax.all_gather(hidden, 'batch', axis=0, tiled=True)  51.1 us
    all_gather x1, waiting for transfers between devices, per_device(): lax.all_gather(attended, 'batch', axis=0, tiled=True)  47.6 us
    all_gather x1, waiting for transfers between devices, per_device(): lax.all_gather(head_norm(own_query, head_dim, query_gain), 'batch', axis=...  46.9 us
    reduce_scatter x1, waiting for transfers between devices, per_device(): lax.psum_scatter(down_part, 'tensor', scatter_dimension=0, tiled=True)  37.6 us
    all_gather x1, waiting for transfers between devices, per_device(): lax.all_gather(part, 'batch', axis=0, tiled=True)  25.7 us
  transfers between devices with their start and end apart: 8, of which 8 were waited for; matrix products, arithmetic and copies ran while one was open for 0% of the time, Pallas kernels for 0%

commit v1 on v0

v1 whole, which is shorter than its diff:
```python
import math

import jax
import jax.numpy as jnp
from jax import lax
from jax.sharding import Mesh, PartitionSpec as P

EPS = 1e-05
ABSENT = -1e30
BF16, F32 = jnp.bfloat16, jnp.float32
SWAP = [(0, 1), (1, 0)]


def swap(value):
    return lax.ppermute(value, "core", SWAP)


def keep_and_send(value, core, axis):
    half = value.shape[axis] // 2
    mine = lax.dynamic_slice_in_dim(value, core * half, half, axis)
    theirs = lax.dynamic_slice_in_dim(value, (1 - core) * half, half, axis)
    return mine, theirs


def share_columns(weight, core):
    mine, theirs = keep_and_send(weight, core, 1)
    return jnp.concatenate([mine, swap(theirs)], axis=0)


def share_rows(weight, core):
    mine, theirs = keep_and_send(weight, core, 0)
    return mine, swap(theirs)


def exchange(value, axis):
    return lax.all_to_all(value, axis, 0, 0, tiled=True)


def gather(value, axis):
    n = lax.axis_size(axis)
    return exchange(jnp.broadcast_to(value[None], (n, *value.shape)), axis)


def dot(left, right):
    return jnp.dot(left, right, preferred_element_type=F32)


def attend(listed, queries, image_keys, image_values):
    picked = queries[jnp.maximum(listed, 0)]
    slots, steps, heads, head_dim = picked.shape
    rows = picked.reshape(slots * steps * heads, head_dim)
    scores = lax.dot_general(rows, image_keys, (((1,), (1,)), ((), ())), preferred_element_type=F32)
    scores = scores * (1.0 / math.sqrt(head_dim))
    top = jnp.max(scores, axis=-1, keepdims=True)
    weights = jnp.exp(scores - top)
    total = jnp.sum(weights, axis=-1, keepdims=True)
    part = (dot(weights.astype(BF16), image_values) / total).astype(BF16)
    lse = top + jnp.log(total)
    return part.reshape(picked.shape), lse.reshape(slots, steps, heads)


def by_request(listed, part, lse, reqs):
    slots, steps, heads, head_dim = part.shape
    hit = jnp.arange(reqs)[:, None] == listed[None, :]
    dense = dot(hit.astype(BF16), part.reshape(slots, -1)).reshape(reqs, steps, heads, head_dim)
    level = jnp.sum(jnp.where(hit[:, :, None, None], lse[None], 0.0), axis=1)
    level = jnp.where(jnp.any(hit, axis=1)[:, None, None], level, ABSENT)
    return dense, level


def per_device(
    tokens, attn_gain, w_query, query_gain, keys, values, w_out, ffn_gain, w_gate, w_up, w_down, citers
):
    core = lax.axis_index("core")
    n_chip, n_tensor = lax.axis_size("chip"), lax.axis_size("tensor")
    steps, reqs, width = tokens.shape
    rows = reqs * steps
    full_width = width * 2 * n_chip
    head_dim = query_gain.shape[0]
    chip_rows = rows // n_chip

    rows_x = jnp.transpose(tokens, (1, 0, 2)).reshape(rows, width)
    normed = (rows_x.astype(F32) * attn_gain.astype(F32)).astype(BF16)
    normed = jnp.concatenate([normed, swap(normed)], axis=1)
    wq = share_columns(w_query, core)
    other_keys, other_values, other_citers = swap(keys[0, 0]), swap(values[0, 0]), swap(citers)
    wo_own, wo_other = share_rows(w_out, core)
    wg, wu = share_columns(w_gate, core), share_columns(w_up, core)
    wd_own, wd_other = share_rows(w_down, core)
    other_gain = swap(ffn_gain)

    query = dot(normed, wq).astype(BF16)
    query = exchange(query.reshape(n_chip, chip_rows, -1), "chip")
    query = jnp.sum(query.astype(F32), axis=0).reshape(chip_rows, -1, head_dim)
    power = jnp.mean(query * query, axis=-1, keepdims=True)
    query = (query * lax.rsqrt(power + EPS) * query_gain.astype(F32)).astype(BF16)
    heads = query.shape[1]
    queries = gather(query.reshape(chip_rows, -1), "chip").reshape(reqs, steps, heads, head_dim)

    one, level_one = by_request(citers[0], *attend(citers[0], queries, keys[0, 0], values[0, 0]), reqs)
    two, level_two = by_request(
        other_citers[0], *attend(other_citers[0], queries, other_keys, other_values), reqs
    )
    peak = jnp.maximum(level_one, level_two)
    weigh_one, weigh_two = jnp.exp(level_one - peak), jnp.exp(level_two - peak)
    total = weigh_one + weigh_two
    part = one * (weigh_one / total)[..., None] + two * (weigh_two / total)[..., None]
    level = jnp.where(peak > 0.5 * ABSENT, peak + jnp.log(total), ABSENT)
    high = lax.optimization_barrier(level.astype(BF16))
    low = (level - high.astype(F32)).astype(BF16)
    pad = jnp.zeros((rows, 128 - 2 * heads), BF16)
    message = jnp.concatenate(
        [part.astype(BF16).reshape(rows, -1), high.reshape(rows, heads), low.reshape(rows, heads), pad],
        axis=1,
    )
    message = exchange(message.reshape(n_chip, chip_rows, -1), "chip")
    columns = heads * head_dim
    part = message[..., :columns].astype(F32).reshape(n_chip, chip_rows, heads, head_dim)
    level = (
        message[..., columns : columns + heads].astype(F32)
        + message[..., columns + heads : columns + 2 * heads].astype(F32)
    )
    share = jnp.exp(level - jnp.max(level, axis=0, keepdims=True))
    share = share / jnp.sum(share, axis=0, keepdims=True)
    attended = jnp.sum(share[..., None] * part, axis=0).reshape(chip_rows, columns).astype(BF16)
    attended = gather(attended, "chip").reshape(rows, columns)

    part_own = dot(attended, wo_own) + swap(dot(attended, wo_other).astype(BF16)).astype(F32)
    part_own = exchange(part_own.astype(BF16).reshape(n_tensor, rows // n_tensor, width), "tensor")
    own_rows = rows // n_tensor
    resid = lax.dynamic_slice_in_dim(rows_x, lax.axis_index("tensor") * own_rows, own_rows, 0)
    resid = resid.astype(F32) + jnp.sum(part_own.astype(F32), axis=0)

    gain = ffn_gain.astype(F32)
    scaled = gather((resid * gain).astype(BF16), "tensor").reshape(rows, width)
    scaled = jnp.concatenate([scaled, swap(scaled)], axis=1)
    both_gain = jnp.concatenate([ffn_gain, other_gain]).astype(F32)
    plain = scaled.astype(F32) / both_gain
    squares = jnp.sum(plain * plain, axis=-1, keepdims=True)
    sq_high = lax.optimization_barrier(squares.astype(BF16))
    sq_low = (squares - sq_high.astype(F32)).astype(BF16)
    sums = jnp.concatenate(
        [dot(scaled, wg).astype(BF16), dot(scaled, wu).astype(BF16), sq_high, sq_low, jnp.zeros((rows, 126), BF16)],
        axis=1,
    )
    sums = exchange(sums.reshape(n_chip, chip_rows, -1), "chip")
    sums = jnp.sum(sums.astype(F32), axis=0)
    units = wg.shape[1]
    squares = sums[:, 2 * units : 2 * units + 1] + sums[:, 2 * units + 1 : 2 * units + 2]
    scale = lax.rsqrt(squares / full_width + EPS)
    gate, up = sums[:, :units] * scale, sums[:, units : 2 * units] * scale
    hidden = (jax.nn.silu(gate) * up).astype(BF16)
    hidden = gather(hidden, "chip").reshape(rows, units)
    down = dot(hidden, wd_own) + swap(dot(hidden, wd_other).astype(BF16)).astype(F32)
    down = exchange(down.astype(BF16).reshape(n_tensor, own_rows, width), "tensor")
    mixed = (resid + jnp.sum(down.astype(F32), axis=0)).astype(BF16)
    return jnp.transpose(mixed.reshape(reqs // n_tensor, steps, width), (1, 0, 2))


def solution(mesh):
    n_batch, n_tensor = mesh.devices.shape
    pairs = Mesh(mesh.devices.reshape(n_batch // 2, 2, n_tensor), ("chip", "core", "tensor"))
    batch = ("chip", "core")
    mapped = jax.shard_map(
        per_device,
        mesh=pairs,
        in_specs=(
            P(None, None, batch),
            P(batch),
            P(batch, "tensor"),
            P(),
            P(batch, "tensor", None, None),
            P(batch, "tensor", None, None),
            P("tensor", batch),
            P(batch),
            P(batch, "tensor"),
            P(batch, "tensor"),
            P("tensor", batch),
            P(batch, None),
        ),
        out_specs=P(None, "tensor", batch),
        check_vma=False,
    )

    def run(*args):
        return mapped(*args[:12])

    return run
```

time: 672 us -> 253 us (0.38)
  waiting for transfers between devices: 532 us -> 71.2 us
  starting transfers between devices: 0.33 us -> 40.1 us
  between operations: 14.4 us -> 0.56 us
  local copies, waits for them, and re-layouts: 11 us -> 23.7 us
  other arithmetic: 15.1 us -> 8.22 us
    unnamed x10 -> x0, waiting for transfers between devices: 250 us -> none
    all_gather x4 -> x0, waiting for transfers between devices: 171 us -> none  [the longest x1 51.1 us: per_device(): lax.all_gather(hidden, 'batch', axis=0, tiled=True)]
    all_to_all x0 -> x3, blocking collectives: none -> 80.6 us  [exchange(): return lax.all_to_all(value, axis, 0, 0, tiled=True)]
    psum x1 -> x0, waiting for transfers between devices: 73.3 us -> none  [per_device(): attn_out = lax.psum(heads_part, 'tensor')]
    all_to_all x0 -> x6, waiting for transfers between devices: none -> 64.4 us  [exchange(): return lax.all_to_all(value, axis, 0, 0, tiled=True)]
    psum x1 -> x0, blocking collectives: 53.2 us -> none  [per_device(): second_sq = lax.psum(jnp.sum(resid * resid, axis=-1), 'batch')]
    reduce_scatter x1 -> x0, waiting for transfers between devices: 37.6 us -> none  [per_device(): lax.psum_scatter(down_part, 'tensor', scatter_dimension=0, tiled=True)]
    all_to_all x0 -> x6, starting transfers between devices: none -> 37.2 us  [exchange(): return lax.all_to_all(value, axis, 0, 0, tiled=True)]
  transfers between devices with their start and end apart: 8 -> 19, of which waited for: 8 -> 11; matrix products, arithmetic and copies ran while one was open for 0% -> 11% of each run, Pallas kernels for 0% -> 0%
where the time goes in v1:
time: 253 us; the launch traced here: 249 us
  blocking collectives  80.6 us (32%)
  waiting for transfers between devices  71.2 us (28%)
  starting transfers between devices  40.1 us (16%)
  matrix products  24.5 us (10%)
  local copies, waits for them, and re-layouts  23.7 us (9%)
  other arithmetic  8.22 us (3%)
    all_to_all x3, blocking collectives, exchange(): return lax.all_to_all(value, axis, 0, 0, tiled=True)  80.6 us
    all_to_all x6, waiting for transfers between devices, exchange(): return lax.all_to_all(value, axis, 0, 0, tiled=True)  64.4 us
    all_to_all x6, starting transfers between devices, exchange(): return lax.all_to_all(value, axis, 0, 0, tiled=True)  37.2 us
    dot_general x11, matrix products, dot(): return jnp.dot(left, right, preferred_element_type=F32)  19.6 us
    ppermute x13, waiting for transfers between devices, swap(): return lax.ppermute(value, 'core', SWAP)  6.77 us
    concatenate x1, local copies, waits for them, and re-layouts, per_device(): jnp.concatenate([dot(scaled, wg).astype(BF16), dot(scaled, wu).astype(BF1...  6.76 us
    dynamic_slice x3, local copies, waits for them, and re-layouts, keep_and_send(): mine = lax.dynamic_slice_in_dim(value, core * half, half, axis)  5.24 us
  transfers between devices with their start and end apart: 19, of which 11 were waited for; matrix products, arithmetic and copies ran while one was open for 11% of the time, Pallas kernels for 0%

profile of v1, /device:TPU:4, one launch (start us, length us, event | category | flops | bytes accessed | tf_op | source)
XLA Modules:
  0.0 248.8 jit_solution(8899798081274626690)
XLA Ops:
  5.6 7.5 %all-to-all-start = ((bf16[16,32,512]{2,1,0:T(8,128)(2,1)}), bf16[16,32,512]{2,1,0:T(8,128)(2,1)S(1)}, u32[]{:S(2)}, u32[]{:S(2)}) async-start(bf16[16,32,512]{2,1,0:T(8,128)(2,1)} %bitcast.4), calls=%async_computation | async-start | bytes 1048576 | tf_op jit(solution)/shard_map/all_to_all | solution.py:36
  13.3 9.5 %all-to-all-done = bf16[16,32,512]{2,1,0:T(8,128)(2,1)S(1)} async-done(((bf16[16,32,512]{2,1,0:T(8,128)(2,1)}), bf16[16,32,512]{2,1,0:T(8,128)(2,1)S(1)}, u32[]{:S(2)}, u32[]{:S(2)}) %all-to-all-start) | async-done | bytes 524320 | tf_op jit(solution)/shard_map/all_to_all | solution.py:36
  24.1 5.8 %all-to-all-start.1 = ((bf16[16,32,512]{2,1,0:T(8,128)(2,1)}), bf16[16,32,512]{2,1,0:T(8,128)(2,1)S(1)}, u32[]{:S(2)}, u32[]{:S(2)}) async-start(bf16[16,32,512]{2,1,0:T(8,128)(2,1)} %broadcast_in_dim.63), calls=%async_computation.1 | async-start | bytes 1048576 | tf_op jit(solution)/shard_map/all_to_all | solution.py:36
  29.9 8.4 %all-to-all-done.1 = bf16[16,32,512]{2,1,0:T(8,128)(2,1)S(1)} async-done(((bf16[16,32,512]{2,1,0:T(8,128)(2,1)}), bf16[16,32,512]{2,1,0:T(8,128)(2,1)S(1)}, u32[]{:S(2)}, u32[]{:S(2)}) %all-to-all-start.1) | async-done | bytes 524320 | tf_op jit(solution)/shard_map/all_to_all | solution.py:36
  39.7 2.5 fusion.68
  43.1 2.5 %fusion.21 = bf16[240,128]{1,0:T(8,128)(2,1)S(1)} fusion(f32[240,6400]{1,0:T(8,128)S(1)} %get-tuple-element.22, f32[240]{0:T(256)S(1)} %get-tuple-element.21, f32[240]{0:T(256)S(1)} %fusion, bf16[1,1,6400,128]{3,2,1,0:T(8,128)(2,1)} %param.19), kind=kOutput, calls=%fused_computation.31 | convolution fusion | flops 396349440 | bytes 7845760 | tf_op jit(solution)/shard_map/dot_general | solution.py:45
  45.9 2.5 fusion.67
  49.4 2.5 %fusion.27 = bf16[240,128]{1,0:T(8,128)(2,1)S(1)} fusion(bf16[6400,128]{1,0:T(8,128)(2,1)} %collective-permute-done.4, f32[240,6400]{1,0:T(8,128)S(1)} %get-tuple-element.20, f32[240]{0:T(256)S(1)} %get-tuple-element.19, f32[240]{0:T(256)S(1)} %fusion.3), kind=kOutput, calls=%fused_computation.33 | convolution fusion | flops 396349440 | bytes 7845760 | tf_op jit(solution)/shard_map/dot_general | solution.py:45
  54.6 14.4 %all_to_all.45 = bf16[16,32,640]{2,1,0:T(8,128)(2,1)S(1)} all-to-all(bf16[16,32,640]{2,1,0:T(8,128)(2,1)S(1)} %maximum_maximum_fusion), channel_id=1, replica_groups=mesh['chip'=16,'core'=2,'tensor'=8] {'chip'}, dimensions={0} | all-to-all | bytes 1310720 | tf_op jit(solution)/shard_map/all_to_all | solution.py:36
  73.6 5.7 %all-to-all-start.3 = ((bf16[16,32,512]{2,1,0:T(8,128)(2,1)}), bf16[16,32,512]{2,1,0:T(8,128)(2,1)S(1)}, u32[]{:S(2)}, u32[]{:S(2)}) async-start(bf16[16,32,512]{2,1,0:T(8,128)(2,1)} %broadcast_in_dim.113), calls=%async_computation.3 | async-start | bytes 1048576 | tf_op jit(solution)/shard_map/all_to_all | solution.py:36
  81.0 6.1 %all-to-all-done.3 = bf16[16,32,512]{2,1,0:T(8,128)(2,1)S(1)} async-done(((bf16[16,32,512]{2,1,0:T(8,128)(2,1)}), bf16[16,32,512]{2,1,0:T(8,128)(2,1)S(1)}, u32[]{:S(2)}, u32[]{:S(2)}) %all-to-all-start.3) | async-done | bytes 524320 | tf_op jit(solution)/shard_map/all_to_all | solution.py:36
  89.9 8.5 %all-to-all-start.4 = ((bf16[8,64,256]{2,1,0:T(8,128)(2,1)}), bf16[8,64,256]{2,1,0:T(8,128)(2,1)S(1)}, u32[]{:S(2)}, u32[]{:S(2)}) async-start(bf16[8,64,256]{2,1,0:T(8,128)(2,1)} %bitcast.20), calls=%async_computation.4 | async-start | bytes 524288 | tf_op jit(solution)/shard_map/all_to_all | solution.py:36
  98.4 12.2 %all-to-all-done.4 = bf16[8,64,256]{2,1,0:T(8,128)(2,1)S(1)} async-done(((bf16[8,64,256]{2,1,0:T(8,128)(2,1)}), bf16[8,64,256]{2,1,0:T(8,128)(2,1)S(1)}, u32[]{:S(2)}, u32[]{:S(2)}) %all-to-all-start.4) | async-done | bytes 262176 | tf_op jit(solution)/shard_map/all_to_all | solution.py:36
  112.1 3.4 %all-to-all-start.5 = ((bf16[8,64,256]{2,1,0:T(8,128)(2,1)}), bf16[8,64,256]{2,1,0:T(8,128)(2,1)S(1)}, u32[]{:S(2)}, u32[]{:S(2)}) async-start(bf16[8,64,256]{2,1,0:T(8,128)(2,1)} %broadcast_in_dim.114), calls=%async_computation.5 | async-start | bytes 524288 | tf_op jit(solution)/shard_map/all_to_all | solution.py:36
  115.5 3.0 %constant_dynamic-slice_fusion.2 = (bf16[256,1792]{1,0:T(8,128)(2,1)}, bf16[256,1792]{1,0:T(8,128)(2,1)}) fusion(bf16[256,3584]{1,0:T(8,128)(2,1)} %param.23, s32[]{:T(128)S(6)} %select_n.63, s32[]{:T(128)S(6)} %select_n.64), kind=kLoop, calls=%fused_computation.99 | loop fusion | bytes 3670024 | tf_op jit(solution)/shard_map/dynamic_slice | solution.py:20
  120.1 6.4 %all-to-all-done.5 = bf16[8,64,256]{2,1,0:T(8,128)(2,1)S(1)} async-done(((bf16[8,64,256]{2,1,0:T(8,128)(2,1)}), bf16[8,64,256]{2,1,0:T(8,128)(2,1)S(1)}, u32[]{:S(2)}, u32[]{:S(2)}) %all-to-all-start.5) | async-done | bytes 262176 | tf_op jit(solution)/shard_map/all_to_all | solution.py:36
  129.2 3.9 %convolution_convert_fusion = bf16[512,1792]{1,0:T(8,128)(2,1)} fusion(bf16[256,1792]{1,0:T(8,128)(2,1)} %collective-permute-done.9, bf16[256,1792]{1,0:T(8,128)(2,1)} %get-tuple-element.7, bf16[512,256]{1,0:T(8,128)(2,1)} %copy-done.4, bf16[512,256]{1,0:T(8,128)(2,1)S(1)} %bitcast.68), kind=kOutput, calls=%fused_computation.15 | convolution fusion | flops 945160192 | bytes 4194304 | tf_op jit(solution)/shard_map/dot_general | solution.py:45
  133.2 3.6 %convolution_convert_fusion.1 = bf16[512,1792]{1,0:T(8,128)(2,1)} fusion(bf16[256,1792]{1,0:T(8,128)(2,1)} %collective-permute-done.8, bf16[256,1792]{1,0:T(8,128)(2,1)S(1)} %get-tuple-element.9, bf16[512,256]{1,0:T(8,128)(2,1)S(1)} %copy-done.5, bf16[512,256]{1,0:T(8,128)(2,1)S(1)} %bitcast.69), kind=kOutput, calls=%fused_computation.16 | convolution fusion | flops 945160192 | bytes 4194304 | tf_op jit(solution)/shard_map/dot_general | solution.py:45
  136.7 6.8 %concatenate.45 = bf16[512,3712]{1,0:T(8,128)(2,1)} concatenate(bf16[512,1792]{1,0:T(8,128)(2,1)} %convolution_convert_fusion.1, bf16[512,1792]{1,0:T(8,128)(2,1)} %convolution_convert_fusion, bf16[512,1]{1,0:T(8,128)(2,1)S(1)} %copy.91, bf16[512,1]{1,0:T(8,128)(2,1)S(1)} %copy.92, bf16[512,126]{1,0:T(8,128)(2,1)S(1)} %broadcast_in_dim.115), dimensions={1} | concatenate | bytes 7602176 | tf_op jit(solution)/shard_map/concatenate | solution.py:142
  143.5 51.0 %all_to_all.46 = bf16[16,32,3712]{2,1,0:T(8,128)(2,1)S(1)} all-to-all(bf16[16,32,3712]{2,1,0:T(8,128)(2,1)} %bitcast.63), channel_id=1, replica_groups=mesh['chip'=16,'core'=2,'tensor'=8] {'chip'}, dimensions={0} | all-to-all | bytes 7602176 | tf_op jit(solution)/shard_map/all_to_all | solution.py:36
  196.8 6.4 %all-to-all-start.7 = ((bf16[16,32,1792]{2,1,0:T(8,128)(2,1)}), bf16[16,32,1792]{2,1,0:T(8,128)(2,1)}, u32[]{:S(2)}, u32[]{:S(2)}) async-start(bf16[16,32,1792]{2,1,0:T(8,128)(2,1)} %broadcast_in_dim.116), calls=%async_computation.7 | async-start | bytes 3670016 | tf_op jit(solution)/shard_map/all_to_all | solution.py:36
  203.3 2.5 collective-permute-done.11
  205.8 21.9 %all-to-all-done.7 = bf16[16,32,1792]{2,1,0:T(8,128)(2,1)} async-done(((bf16[16,32,1792]{2,1,0:T(8,128)(2,1)}), bf16[16,32,1792]{2,1,0:T(8,128)(2,1)}, u32[]{:S(2)}, u32[]{:S(2)}) %all-to-all-start.7) | async-done | bytes 1835040 | tf_op jit(solution)/shard_map/all_to_all | solution.py:36
  232.1 15.2 %all_to_all.47 = bf16[8,64,256]{2,1,0:T(8,128)(2,1)S(1)} all-to-all(bf16[8,64,256]{2,1,0:T(8,128)(2,1)S(1)} %bitcast.70), channel_id=1, replica_groups=mesh['chip'=16,'core'=2,'tensor'=8] {'tensor'}, dimensions={0} | all-to-all | bytes 524288 | tf_op jit(solution)/shard_map/all_to_all | solution.py:36
  (127 shorter events, 36.4 us)
Async XLA Ops:
  0.0 203.2 %copy-start = (bf16[3584,256]{1,0:T(8,128)(2,1)S(1)}, bf16[3584,256]{1,0:T(8,128)(2,1)}, u32[]{:S(2)}) copy-start(bf16[3584,256]{1,0:T(8,128)(2,1)} %param.24) | copy-start | bytes 5505028
  1.2 2.6 %collective-permute-start.1 = (bf16[256,512]{1,0:T(8,128)(2,1)S(1)}, bf16[256,512]{1,0:T(8,128)(2,1)S(1)}, u32[]{:S(2)}, u32[]{:S(2)}) collective-permute-start(bf16[256,512]{1,0:T(8,128)(2,1)S(1)} %get-tuple-element.12), channel_id=1, source_target_pairs={{0,8},{8,0},{1,9},{9,1},{2,10},{10,2},{3,11},{11,3},{4,12},{12,4},... | collective-permute-start | bytes 786440 | tf_op jit(solution)/shard_map/ppermute | solution.py:15
  2.6 10.5 %copy-start.9 = (bf16[128]{0:T(256)(128)(2,1)S(1)}, bf16[128]{0:T(256)(128)(2,1)}, u32[]{:S(2)}) copy-start(bf16[128]{0:T(256)(128)(2,1)} %param.17) | copy-start | bytes 772
  2.7 1.7 collective-permute-start
  3.2 26.6 %collective-permute-start.2 = (s32[1,15]{1,0:T(1,128)S(1)}, s32[1,15]{1,0:T(1,128)S(1)}, u32[]{:S(2)}, u32[]{:S(2)}) collective-permute-start(s32[1,15]{1,0:T(1,128)S(1)} %copy-done.6), channel_id=1, source_target_pairs={{0,8},{8,0},{1,9},{9,1},{2,10},{10,2},{3,11},{11,3},{4,12},{12,4},... | collective-permute-start | bytes 188 | tf_op jit(solution)/shard_map/ppermute | solution.py:15
  3.3 42.6 %collective-permute-start.3 = (bf16[6400,128]{1,0:T(8,128)(2,1)}, bf16[6400,128]{1,0:T(8,128)(2,1)}, u32[]{:S(2)}, u32[]{:S(2)}) collective-permute-start(bf16[6400,128]{1,0:T(8,128)(2,1)} %bitcast.8), channel_id=1, source_target_pairs={{0,8},{8,0},{1,9},{9,1},{2,10},{10,2},{3,11},{11,3},{4,12},{12,4},... | collective-permute-start | bytes 4915208 | tf_op jit(solution)/shard_map/ppermute | solution.py:15
  3.7 45.7 %collective-permute-start.4 = (bf16[6400,128]{1,0:T(8,128)(2,1)}, bf16[6400,128]{1,0:T(8,128)(2,1)}, u32[]{:S(2)}, u32[]{:S(2)}) collective-permute-start(bf16[6400,128]{1,0:T(8,128)(2,1)} %bitcast.9), channel_id=1, source_target_pairs={{0,8},{8,0},{1,9},{9,1},{2,10},{10,2},{3,11},{11,3},{4,12},{12,4},... | collective-permute-start | bytes 4915208 | tf_op jit(solution)/shard_map/ppermute | solution.py:15
  5.6 17.2 %all-to-all-start = ((bf16[16,32,512]{2,1,0:T(8,128)(2,1)}), bf16[16,32,512]{2,1,0:T(8,128)(2,1)S(1)}, u32[]{:S(2)}, u32[]{:S(2)}) async-start(bf16[16,32,512]{2,1,0:T(8,128)(2,1)} %bitcast.4), calls=%async_computation | async-start | bytes 1048576 | tf_op jit(solution)/shard_map/all_to_all | solution.py:36
  24.1 14.3 %all-to-all-start.1 = ((bf16[16,32,512]{2,1,0:T(8,128)(2,1)}), bf16[16,32,512]{2,1,0:T(8,128)(2,1)S(1)}, u32[]{:S(2)}, u32[]{:S(2)}) async-start(bf16[16,32,512]{2,1,0:T(8,128)(2,1)} %broadcast_in_dim.63), calls=%async_computation.1 | async-start | bytes 1048576 | tf_op jit(solution)/shard_map/all_to_all | solution.py:36
  71.3 8.0 %copy-start.3 = (bf16[1024,256]{1,0:T(8,128)(2,1)S(1)}, bf16[1024,256]{1,0:T(8,128)(2,1)}, u32[]{:S(2)}) copy-start(bf16[1024,256]{1,0:T(8,128)(2,1)} %param.20) | copy-start | bytes 1572868
  73.6 13.4 %all-to-all-start.3 = ((bf16[16,32,512]{2,1,0:T(8,128)(2,1)}), bf16[16,32,512]{2,1,0:T(8,128)(2,1)S(1)}, u32[]{:S(2)}, u32[]{:S(2)}) async-start(bf16[16,32,512]{2,1,0:T(8,128)(2,1)} %broadcast_in_dim.113), calls=%async_computation.3 | async-start | bytes 1048576 | tf_op jit(solution)/shard_map/all_to_all | solution.py:36
  79.3 1.6 collective-permute-start.5
  87.0 11.4 %copy-start.7 = (bf16[256]{0:T(256)(128)(2,1)S(1)}, bf16[256]{0:T(256)(128)(2,1)}, u32[]{:S(2)}) copy-start(bf16[256]{0:T(256)(128)(2,1)} %param.21) | copy-start | bytes 1540
  87.3 1.8 collective-permute-start.6
  89.9 20.6 %all-to-all-start.4 = ((bf16[8,64,256]{2,1,0:T(8,128)(2,1)}), bf16[8,64,256]{2,1,0:T(8,128)(2,1)S(1)}, u32[]{:S(2)}, u32[]{:S(2)}) async-start(bf16[8,64,256]{2,1,0:T(8,128)(2,1)} %bitcast.20), calls=%async_computation.4 | async-start | bytes 524288 | tf_op jit(solution)/shard_map/all_to_all | solution.py:36
  112.1 14.4 %all-to-all-start.5 = ((bf16[8,64,256]{2,1,0:T(8,128)(2,1)}), bf16[8,64,256]{2,1,0:T(8,128)(2,1)S(1)}, u32[]{:S(2)}, u32[]{:S(2)}) async-start(bf16[8,64,256]{2,1,0:T(8,128)(2,1)} %broadcast_in_dim.114), calls=%async_computation.5 | async-start | bytes 524288 | tf_op jit(solution)/shard_map/all_to_all | solution.py:36
  118.5 10.7 %collective-permute-start.9 = (bf16[256,1792]{1,0:T(8,128)(2,1)}, bf16[256,1792]{1,0:T(8,128)(2,1)}, u32[]{:S(2)}, u32[]{:S(2)}) collective-permute-start(bf16[256,1792]{1,0:T(8,128)(2,1)} %get-tuple-element.8), channel_id=1, source_target_pairs={{0,8},{8,0},{1,9},{9,1},{2,10},{10,2},{3,11},{11,3},{4,12},{12,4},... | collective-permute-start | bytes 2752520 | tf_op jit(solution)/shard_map/ppermute | solution.py:15
  119.6 13.5 %collective-permute-start.8 = (bf16[256,1792]{1,0:T(8,128)(2,1)}, bf16[256,1792]{1,0:T(8,128)(2,1)}, u32[]{:S(2)}, u32[]{:S(2)}) collective-permute-start(bf16[256,1792]{1,0:T(8,128)(2,1)} %get-tuple-element.10), channel_id=1, source_target_pairs={{0,8},{8,0},{1,9},{9,1},{2,10},{10,2},{3,11},{11,3},{4,12},{12,4},... | collective-permute-start | bytes 2752520 | tf_op jit(solution)/shard_map/ppermute | solution.py:15
  126.5 1.5 collective-permute-start.7
  126.5 1.5 collective-permute-start.10
  129.2 4.0 %copy-start.5 = (bf16[512,256]{1,0:T(8,128)(2,1)S(1)}, bf16[512,256]{1,0:T(8,128)(2,1)}, u32[]{:S(2)}) copy-start(bf16[512,256]{1,0:T(8,128)(2,1)} %copy-done.4) | copy-start | bytes 786436
  196.8 30.9 %all-to-all-start.7 = ((bf16[16,32,1792]{2,1,0:T(8,128)(2,1)}), bf16[16,32,1792]{2,1,0:T(8,128)(2,1)}, u32[]{:S(2)}, u32[]{:S(2)}) async-start(bf16[16,32,1792]{2,1,0:T(8,128)(2,1)} %broadcast_in_dim.116), calls=%async_computation.7 | async-start | bytes 3670016 | tf_op jit(solution)/shard_map/all_to_all | solution.py:36
  203.2 2.6 %collective-permute-start.11 = (bf16[1792,256]{1,0:T(8,128)(2,1)S(1)}, bf16[1792,256]{1,0:T(8,128)(2,1)S(1)}, u32[]{:S(2)}, u32[]{:S(2)}) collective-permute-start(bf16[1792,256]{1,0:T(8,128)(2,1)S(1)} %constant_dynamic-slice_fusion), channel_id=1, source_target_pairs={{0,8},{8,0},{1,9},{9,1},{2,10},{10,2},{3,11},{11,3},{4,12},{12,4},... | collective-permute-start | bytes 2752520 | tf_op jit(solution)/shard_map/ppermute | solution.py:15
  229.8 2.3 collective-permute-start.12
  (5 other events, 12.5 us)
